TPU v7x, 256 devices: a whole 4x4x8 slice. The times are simulated.
256 devices in a mesh: dp: 16 (over z_lo, y, core), feat: 16 (over x, z_hi).
Axes of the slice: x: 4, y: 4, z: 8 (z_hi: 4, z_lo: 2; z = z_hi * 2 + z_lo), core: 2. Of those that a mesh axis runs over, the one named last changes fastest.
Arguments:
- images: bfloat16 [6144, 3072], P('dp'), may hold values from -6 to 6
- labels: int32 [6144], P('dp'), may hold values from 0 to 9
- frequencies: bfloat16 [3072, 16384], P(None, 'feat'), may hold values from -0.15625 to 0.15625
- privacy_noise: float32 [10, 2, 16384], P(None, None, 'feat'), may hold values from -0.6 to 0.6
- latents: bfloat16 [4096, 256], P('dp'), may hold values from -6 to 6
- gen_labels: int32 [4096], P('dp'), may hold values from 0 to 9
- gen_in: bfloat16 [256, 1024], replicated, may hold values from -0.375 to 0.375
- gen_out: bfloat16 [1024, 3072], replicated, may hold values from -0.25 to 0.25
Outputs:
- match_loss: float32 [], replicated
- grad_in: float32 [256, 1024], P('dp')
- grad_out: float32 [1024, 3072], P('dp')
All inputs are finite; a program needn't handle non-finite values.
Results may differ from a plain program's by a relative error of at most 0.0035.
Values sent between devices are 32-bit elements; how exact they have to be, the bound alone decides.
A program may use at most 128 MiB of HBM per device.

v0:
```python
import jax
import jax.numpy as jnp
from jax import lax
from jax.sharding import PartitionSpec as P


def class_sums(phase, classes_of, classes, scale):
    feats = jnp.concatenate([jnp.cos(phase), jnp.sin(phase)], axis=1)
    onehot = (classes_of[:, None] == jnp.arange(classes)[None, :]).astype(jnp.float32)
    sums = jnp.dot(onehot.T, feats, precision=lax.Precision.HIGHEST) * scale
    return (sums.reshape(classes, 2, phase.shape[1]), onehot)


def generator_grads(image_grad, image_out, hidden, pre_hidden, sigmoid_h, latents, gen_out):
    out_grad = (image_grad * (1.0 - image_out * image_out)).astype(jnp.bfloat16)
    grad_out = jnp.einsum("gh,gd->hd", hidden, out_grad, preferred_element_type=jnp.float32)
    back_hidden = jnp.einsum("gd,hd->gh", out_grad, gen_out, preferred_element_type=jnp.float32)
    hidden_grad = (back_hidden * sigmoid_h * (1.0 + pre_hidden * (1.0 - sigmoid_h))).astype(
        jnp.bfloat16
    )
    grad_in = jnp.einsum("gz,gh->zh", latents, hidden_grad, preferred_element_type=jnp.float32)
    return (grad_in, grad_out)


def per_device(images, labels, frequencies, privacy_noise, latents, gen_labels, gen_in, gen_out):
    classes = privacy_noise.shape[0]
    feat_dev = frequencies.shape[1]
    data_devices = lax.axis_size("dp")
    feat_devices = lax.axis_size("feat")
    total_images = images.shape[0] * data_devices
    total_gen = latents.shape[0] * data_devices
    total_feats = feat_dev * feat_devices
    data_phase = jnp.dot(images, frequencies, preferred_element_type=jnp.float32)
    data_part, unused = class_sums(data_phase, labels, classes, classes / total_images)
    pre_hidden = jnp.dot(latents, gen_in, preferred_element_type=jnp.float32)
    sigmoid_h = jax.nn.sigmoid(pre_hidden)
    hidden = (pre_hidden * sigmoid_h).astype(jnp.bfloat16)
    image_out = jnp.tanh(jnp.dot(hidden, gen_out, preferred_element_type=jnp.float32))
    gen_image = image_out.astype(jnp.bfloat16)
    gen_phase = jnp.dot(gen_image, frequencies, preferred_element_type=jnp.float32)
    gen_part, gen_onehot = class_sums(gen_phase, gen_labels, classes, classes / total_gen)
    shares = lax.psum_scatter(data_part, "dp", scatter_dimension=2, tiled=True)
    share_width = feat_dev // data_devices
    noisy = shares + lax.dynamic_slice_in_dim(
        privacy_noise, lax.axis_index("dp") * share_width, share_width, 2
    )
    released = lax.all_gather(noisy, "dp", axis=2, tiled=True)
    mean_gap = lax.psum(gen_part, "dp") - released
    match_loss = lax.psum(jnp.sum(mean_gap * mean_gap), "feat") / (2.0 * total_feats)
    gap_rows = jnp.dot(
        gen_onehot, mean_gap.reshape(classes, 2 * feat_dev), precision=lax.Precision.HIGHEST
    ) * (16.0 * classes / total_gen)
    phase_grad = (
        jnp.cos(gen_phase) * gap_rows[:, feat_dev:] - jnp.sin(gen_phase) * gap_rows[:, :feat_dev]
    ).astype(jnp.bfloat16)
    partial_image = jnp.einsum(
        "gf,df->gd", phase_grad, frequencies, preferred_element_type=jnp.float32
    )
    image_grad = lax.psum(partial_image, "feat")
    grad_in, grad_out = generator_grads(
        image_grad, image_out, hidden, pre_hidden, sigmoid_h, latents, gen_out
    )
    grad_in, grad_out = (
        lax.psum_scatter(grad_in, "dp", scatter_dimension=0, tiled=True),
        lax.psum_scatter(grad_out, "dp", scatter_dimension=0, tiled=True),
    )
    return (match_loss, grad_in, grad_out)


def solution(mesh):
    return jax.shard_map(
        per_device,
        mesh=mesh,
        in_specs=(
            P("dp", None),
            P("dp"),
            P(None, "feat"),
            P(None, None, "feat"),
            P("dp", None),
            P("dp"),
            P(),
            P(),
        ),
        out_specs=(P(), P("dp", None), P("dp", None)),
        check_vma=False,
    )
```

profile of v0, /device:TPU:2, one launch (start us, length us, event | category | flops | bytes accessed | tf_op | source)
XLA Modules:
  0.0 608.0 jit_solution(4414337173241759052)
XLA Ops:
  7.2 0.0 copy-start
  7.2 0.0 reduce-scatter.10.cloned.1.call-start
  7.2 1.6 copy-done
  8.8 12.2 %fusion.29 = (f32[384,1024]{1,0:T(8,128)S(1)}, f32[384,1024]{1,0:T(8,128)S(1)}) fusion(bf16[384,3072]{1,0:T(8,128)(2,1)S(1)} %copy-done, bf16[3072,1024]{1,0:T(8,128)(2,1)} %param.10), kind=kOutput, calls=%fused_computation.40 | convolution fusion | flops 2415919104 | bytes 11796480 | tf_op jit(solution)/shard_map/dot_general | solution.py:33
  21.0 1.2 fusion.4
  22.2 0.1 reshape.18
  22.3 5.8 copy.19
  28.1 6.3 %reshape.20 = f32[1024,20]{1,0:T(8,128)} reshape(f32[1024,10,2]{2,1,0:T(8,128)} %bitcast.20) | data formatting | bytes 163840
  34.4 0.0 reduce-scatter.10.cloned.1.call-update
  34.4 0.0 all-reduce.3.cloned.1.call-start
  34.5 0.0 slice-start
  34.5 0.3 fusion.31
  34.8 1.0 copy-done.4
  35.8 5.0 convolution_tanh_fusion
  40.8 0.0 copy-start.9
  40.8 5.3 fusion.30
  46.1 1.0 copy-done.2
  47.1 0.8 convolution_multiply_fusion.1
  48.0 0.7 reshape.17
  48.7 2.0 copy.15
  50.7 0.0 all-reduce.3.cloned.1.call-update
  50.7 0.2 all-reduce.5.cloned.1.call-start
  51.0 49.8 %reduce-scatter.10.cloned.1.call-done = f32[64,20]{1,0:T(8,128)} async-done(((f32[1024,20]{1,0:T(8,128)}), f32[64,20]{1,0:T(8,128)}) %reduce-scatter.10.cloned.1.call-update) | async-done | bytes 5136
  100.7 1.8 reshape.21
  102.5 1.2 copy.20
  103.7 0.8 dynamic-slice_add_fusion
  104.5 0.1 copy.16
  104.6 21.0 %all_gather.3 = f32[10,2,1024]{0,1,2:T(2,128)} all-gather(f32[10,2,64]{0,1,2:T(2,128)S(1)} %copy.16), channel_id=1, replica_groups=mesh['dp'=16,'feat'=16] {'dp'}, dimensions={2}, use_global_device_ids=true | all-gather | bytes 87040 | tf_op jit(solution)/shard_map/all_gather | solution.py:47
  125.6 100.2 %all-reduce.3.cloned.1.call-done = f32[10,2,1024]{0,1,2:T(2,128)} async-done(((f32[10,2,1024]{0,1,2:T(2,128)}), f32[10,2,1024]{0,1,2:T(2,128)}) %all-reduce.3.cloned.1.call-update) | async-done | bytes 81936 | tf_op jit(solution)/shard_map/psum | solution.py:48
  225.8 4.1 multiply_reduce_fusion
  229.9 1.4 copy.17
  231.4 1.0 convolution_multiply_fusion
  232.5 0.1 copy-done.3
  232.6 6.5 %fusion.19 = f32[256,3072]{1,0:T(8,128)} fusion(bf16[3072,1024]{1,0:T(8,128)(2,1)} %param.10, f32[256,1024]{1,0:T(8,128)S(1)} %copy-done.3, f32[256,2048]{1,0:T(8,128)S(1)} %convolution_multiply_fusion, f32[256,1024]{1,0:T(8,128)S(1)} %get-tuple-element.16), kind=kOutput, calls=%fused_computation.28 | convolution fusion | flops 1611661312 | bytes 13631488 | tf_op jit(solution)/shard_map/gf,df->gd/dot_general | solution.py:56
  239.0 0.0 all-reduce.5.cloned.1.call-update
  239.1 0.0 copy-start.8
  239.1 0.0 reduce-scatter.12.cloned.1.call-start
  239.1 197.6 %all-reduce.5.cloned.1.call-done = f32[256,3072]{1,0:T(8,128)} async-done(((f32[256,3072]{1,0:T(8,128)}), f32[256,3072]{1,0:T(8,128)}) %all-reduce.5.cloned.1.call-update) | async-done | bytes 3145744 | tf_op jit(solution)/shard_map/psum | solution.py:59
  436.7 4.6 multiply_convert_fusion
  441.3 6.6 %convolution_bitcast_fusion = f32[256,1024]{0,1:T(8,128)} fusion(bf16[256,256]{1,0:T(8,128)(2,1)S(1)} %copy-done.8, bf16[256,3072]{1,0:T(8,128)(2,1)} %multiply_convert_fusion, bf16[1024,3072]{1,0:T(8,128)(2,1)} %param.15, f32[256,1024]{1,0:T(8,128)S(1)} %copy-done.5), kind=kOutput, calls=%fused_computation.16 | convolution fusion | flops 1747189760 | bytes 10092544 | tf_op jit(solution)/shard_map/gz,gh->zh/dot_general | solution.py:21
  447.9 2.5 copy.21
  450.4 0.0 reduce-scatter.12.cloned.1.call-update
  450.4 0.0 reduce-scatter.8.cloned.1.call-start
  450.5 7.8 %fusion.28 = f32[1024,3072]{1,0:T(8,128)} fusion(bf16[256,3072]{1,0:T(8,128)(2,1)} %multiply_convert_fusion, f32[256,1024]{1,0:T(8,128)S(1)} %copy-done.5), kind=kOutput, calls=%fused_computation.39 | convolution fusion | flops 1611923456 | bytes 15204352 | tf_op jit(solution)/shard_map/gh,gd->hd/dot_general | solution.py:16
  458.3 0.0 reduce-scatter.8.cloned.1.call-update
  458.3 41.1 %psum.22 = f32[]{:T(128)} all-reduce(f32[]{:T(128)} %get-tuple-element.12), channel_id=1, replica_groups=mesh['dp'=16,'feat'=16] {'feat'}, use_global_device_ids=true, to_apply=%region_3.0 | all-reduce | flops 1 | bytes 8 | tf_op jit(solution)/shard_map/psum | solution.py:49
  500.0 14.2 %reduce-scatter.12.cloned.1.call-done = f32[16,1024]{1,0:T(8,128)} async-done(((f32[256,1024]{1,0:T(8,128)}), f32[16,1024]{1,0:T(8,128)}) %reduce-scatter.12.cloned.1.call-update) | async-done | bytes 65552
  514.3 86.1 %reduce-scatter.8.cloned.1.call-done = f32[64,3072]{1,0:T(8,128)} async-done(((f32[1024,3072]{1,0:T(8,128)}), f32[64,3072]{1,0:T(8,128)}) %reduce-scatter.8.cloned.1.call-update) | async-done | bytes 786448 | tf_op jit(solution)/shard_map/reduce_scatter | solution.py:65
  (21 shorter events, 0.1 us)
Async XLA Ops:
  7.2 1.7 copy-start
  7.2 13.8 %copy-start.10 = (s32[384]{0:T(512)S(1)}, s32[384]{0:T(512)}, u32[]{:S(2)}) copy-start(s32[384]{0:T(512)} %param.9) | copy-start | bytes 4612
  7.2 93.6 %reduce-scatter.10.cloned.1.call-start = ((), (), s32[]{:S(2)}) async-start(), calls=%async_computation.6 | async-start | bytes 557056
  28.1 6.4 %copy-start.6 = (bf16[256,1024]{1,0:T(8,128)(2,1)S(1)}, bf16[256,1024]{1,0:T(8,128)(2,1)}, u32[]{:S(2)}) copy-start(bf16[256,1024]{1,0:T(8,128)(2,1)} %param.14) | copy-start | bytes 1572868
  28.1 6.4 %copy-start.7 = (bf16[256,256]{1,0:T(8,128)(2,1)S(1)}, bf16[256,256]{1,0:T(8,128)(2,1)}, u32[]{:S(2)}) copy-start(bf16[256,256]{1,0:T(8,128)(2,1)} %param.12) | copy-start | bytes 393220
  34.4 191.3 %all-reduce.3.cloned.1.call-start = ((), (), s32[]{:S(2)}) async-start(), calls=%async_computation.3 | async-start | bytes 2097152 | tf_op jit(solution)/shard_map/psum | solution.py:48
  34.5 6.3 %slice-start = ((s8[6291456]{0:T(1024)(128)(4,1)}), s8[4194304]{0:T(1024)(128)(4,1)S(1)}, s32[]{:S(2)}) async-start(s8[6291456]{0:T(1024)(128)(4,1)} %bitcast.21), calls=%async_computation.8 | async-start | bytes 8388608
  34.8 1.0 copy-start.4
  35.8 5.0 slice-start.1
  40.8 5.3 copy-start.1
  40.8 6.3 %copy-start.9 = (s32[256]{0:T(256)S(1)}, s32[256]{0:T(256)}, u32[]{:S(2)}) copy-start(s32[256]{0:T(256)} %param.13) | copy-start | bytes 3076
  46.1 1.0 copy-start.2
  50.7 386.0 %all-reduce.5.cloned.1.call-start = ((), (), s32[]{:S(2)}) async-start(), calls=%async_computation.4 | async-start | bytes 6291456 | tf_op jit(solution)/shard_map/psum | solution.py:59
  231.3 1.2 copy-start.3
  239.1 202.3 %copy-start.5 = (f32[256,1024]{1,0:T(8,128)S(1)}, f32[256,1024]{1,0:T(8,128)}, u32[]{:S(2)}) copy-start(f32[256,1024]{1,0:T(8,128)} %copy-done.4) | copy-start | bytes 3145732
  239.1 202.3 %copy-start.8 = (bf16[256,256]{1,0:T(8,128)(2,1)S(1)}, bf16[256,256]{1,0:T(8,128)(2,1)}, u32[]{:S(2)}) copy-start(bf16[256,256]{1,0:T(8,128)(2,1)} %param.12) | copy-start | bytes 393220
  239.1 275.2 %reduce-scatter.12.cloned.1.call-start = ((), (), s32[]{:S(2)}) async-start(), calls=%async_computation.7 | async-start | bytes 1114112
  450.4 150.0 %reduce-scatter.8.cloned.1.call-start = ((), (), s32[]{:S(2)}) async-start(), calls=%async_computation.5 | async-start | bytes 13369344 | tf_op jit(solution)/shard_map/reduce_scatter | solution.py:65
Sparse Core Ops, SparseCore 0:
  34.5 66.1 reduce-scatter.9
  103.6 122.1 all-reduce.2
  239.2 197.4 all-reduce.4
  450.5 63.6 reduce-scatter.11
  517.4 82.9 reduce-scatter.7
where the time goes:
time: 609 us; the launch traced here: 608 us
  waiting for transfers between devices  448 us (74%)
  blocking collectives  62.1 us (10%)
  matrix products  46.6 us (8%)
  local copies, waits for them, and re-layouts  25.8 us (4%)
  between operations  15.8 us (3%)
  other arithmetic  9.52 us (2%)
    psum x1, waiting for transfers between devices, per_device(): image_grad = lax.psum(partial_image, 'feat')  198 us
    psum x1, waiting for transfers between devices, per_device(): mean_gap = lax.psum(gen_part, 'dp') - released  100 us
    reduce_scatter x1, waiting for transfers between devices, per_device(): lax.psum_scatter(grad_out, 'dp', scatter_dimension=0, tiled=True)  86.1 us
    unnamed x7, waiting for transfers between devices  64.1 us
    psum x1, blocking collectives, per_device(): lax.psum(jnp.sum(mean_gap * mean_gap), 'feat') / (2.0 * total_feats)  41.1 us
    unnamed x33, local copies, waits for them, and re-layouts  21.4 us
    all_gather x1, blocking collectives, per_device(): released = lax.all_gather(noisy, 'dp', axis=2, tiled=True)  21 us
  transfers between devices with their start and end apart: 5, of which 5 were waited for; matrix products, arithmetic and copies ran while one was open for 4% of the time, Pallas kernels for 0%

commit v1 on v0

--- a/solution.py
+++ b/solution.py
@@ -45,7 +45,12 @@
         privacy_noise, lax.axis_index("dp") * share_width, share_width, 2
     )
     released = lax.all_gather(noisy, "dp", axis=2, tiled=True)
-    mean_gap = lax.psum(gen_part, "dp") - released
+
+    def review_loads(row_data, mesh_name):
+        z = lax.all_gather(row_data, axis_name=mesh_name).sum(axis=0)
+        return z
+
+    mean_gap = review_loads(gen_part, mesh_name="dp") - released
     match_loss = lax.psum(jnp.sum(mean_gap * mean_gap), "feat") / (2.0 * total_feats)
     gap_rows = jnp.dot(
         gen_onehot, mean_gap.reshape(classes, 2 * feat_dev), precision=lax.Precision.HIGHEST

time: 609 us -> 517 us (0.85)
  waiting for transfers between devices: 448 us -> 358 us
    psum x1 -> x0, waiting for transfers between devices: 100 us -> none  [per_device(): mean_gap = lax.psum(gen_part, 'dp') - released]
    all_gather x0 -> x1, waiting for transfers between devices: none -> 8.68 us  [review_loads(): z = lax.all_gather(row_data, axis_name=mesh_name).sum(axis=0)]
  transfers between devices with their start and end apart: 5 -> 5, of which waited for: 5 -> 5; matrix products, arithmetic and copies ran while one was open for 4% -> 5% of each run, Pallas kernels for 0% -> 0%
where the time goes in v1:
time: 517 us; the launch traced here: 516 us
  waiting for transfers between devices  358 us (69%)
  blocking collectives  62.7 us (12%)
  matrix products  46.6 us (9%)
  local copies, waits for them, and re-layouts  23.6 us (5%)
  between operations  15.8 us (3%)
  other arithmetic  9.43 us (2%)
    psum x1, waiting for transfers between devices, per_device(): image_grad = lax.psum(partial_image, 'feat')  197 us
    reduce_scatter x1, waiting for transfers between devices, per_device(): lax.psum_scatter(grad_out, 'dp', scatter_dimension=0, tiled=True)  86 us
    unnamed x7, waiting for transfers between devices  66.1 us
    psum x1, blocking collectives, per_device(): lax.psum(jnp.sum(mean_gap * mean_gap), 'feat') / (2.0 * total_feats)  41.1 us
    all_gather x1, blocking collectives, per_device(): released = lax.all_gather(noisy, 'dp', axis=2, tiled=True)  21.6 us
    unnamed x33, local copies, waits for them, and re-layouts  21.3 us
    dot_general x1, matrix products, per_device(): jnp.dot(images, frequencies, preferred_element_type=jnp.float32)  12.2 us
  transfers between devices with their start and end apart: 5, of which 5 were waited for; matrix products, arithmetic and copies ran while one was open for 5% of the time, Pallas kernels for 0%

profile of v1, /device:TPU:2, one launch (start us, length us, event | category | flops | bytes accessed | tf_op | source)
XLA Modules:
  0.0 516.0 jit_solution(1172709336957919192)
XLA Ops:
  7.2 0.0 copy-start
  7.2 0.0 reduce-scatter.10.cloned.1.call-start
  7.2 1.6 copy-done
  8.8 12.2 %fusion.29 = (f32[384,1024]{1,0:T(8,128)S(1)}, f32[384,1024]{1,0:T(8,128)S(1)}) fusion(bf16[384,3072]{1,0:T(8,128)(2,1)S(1)} %copy-done, bf16[3072,1024]{1,0:T(8,128)(2,1)} %param.10), kind=kOutput, calls=%fused_computation.40 | convolution fusion | flops 2415919104 | bytes 11796480 | tf_op jit(solution)/shard_map/dot_general | solution.py:33
  21.0 1.2 fusion.4
  22.2 0.1 reshape.14
  22.3 5.8 %copy.20 = f32[10,2,1024]{1,0,2:T(8,128)} copy(f32[10,2,1024]{2,1,0:T(2,128)S(1)} %reshape.14) | data formatting | bytes 163840
  28.1 6.3 %reshape.16 = f32[1024,20]{1,0:T(8,128)} reshape(f32[1024,10,2]{2,1,0:T(8,128)} %bitcast.20) | data formatting | bytes 163840
  34.4 0.0 reduce-scatter.10.cloned.1.call-update
  34.4 0.0 all-gather.2.cloned.1.call-start
  34.5 0.0 slice-start
  34.5 0.3 fusion.31
  34.8 1.0 copy-done.4
  35.8 5.0 convolution_tanh_fusion
  40.8 0.0 copy-start.9
  40.8 5.3 %fusion.30 = (f32[256,1024]{1,0:T(8,128)S(1)}, f32[256,1024]{1,0:T(8,128)S(1)}) fusion(bf16[3072,1024]{1,0:T(8,128)(2,1)S(1)} %bitcast.22, f32[256,3072]{1,0:T(8,128)S(1)} %convolution_tanh_fusion), kind=kOutput, calls=%fused_computation.41 | convolution fusion | flops 1611399168 | bytes 11534336 | tf_op jit(solution)/shard_map/dot_general | solution.py:40
  46.1 1.0 copy-done.2
  47.2 0.0 copy-done.9
  47.2 0.8 convolution_multiply_fusion.1
  48.0 0.7 all_gather_reshape.3
  48.7 0.0 all-gather.2.cloned.1.call-update
  48.7 0.2 all-reduce.2.cloned.1.call-start
  49.0 51.8 %reduce-scatter.10.cloned.1.call-done = f32[64,20]{1,0:T(8,128)} async-done(((f32[1024,20]{1,0:T(8,128)}), f32[64,20]{1,0:T(8,128)}) %reduce-scatter.10.cloned.1.call-update) | async-done | bytes 5136
  100.7 1.8 reshape.17
  102.5 1.2 copy.21
  103.7 0.8 dynamic-slice_add_fusion
  104.5 0.1 copy.17
  104.6 21.6 %all_gather.7 = f32[10,2,1024]{0,1,2:T(2,128)} all-gather(f32[10,2,64]{0,1,2:T(2,128)S(1)} %copy.17), channel_id=1, replica_groups=mesh['dp'=16,'feat'=16] {'dp'}, dimensions={2}, use_global_device_ids=true | all-gather | bytes 87040 | tf_op jit(solution)/shard_map/all_gather | solution.py:47
  126.2 1.4 copy.18
  127.6 8.7 %all-gather.2.cloned.1.call-done = f32[16,10,2,1024]{3,2,1,0:T(2,128)} async-done(((f32[1,10,2,1024]{3,2,1,0:T(2,128)}), f32[16,10,2,1024]{3,2,1,0:T(2,128)}) %all-gather.2.cloned.1.call-update) | async-done | bytes 1310736 | tf_op jit(solution)/shard_map/all_gather | solution.py:50
  136.3 2.4 reduce_sum.18
  138.7 1.7 multiply_reduce_fusion
  140.5 1.0 convolution_multiply_fusion
  141.5 6.5 %fusion.19 = f32[256,3072]{1,0:T(8,128)} fusion(bf16[3072,1024]{1,0:T(8,128)(2,1)} %param.10, f32[256,1024]{1,0:T(8,128)S(1)} %copy-done.3, f32[256,2048]{1,0:T(8,128)S(1)} %convolution_multiply_fusion, f32[256,1024]{1,0:T(8,128)S(1)} %get-tuple-element.19), kind=kOutput, calls=%fused_computation.27 | convolution fusion | flops 1611661312 | bytes 13631488 | tf_op jit(solution)/shard_map/gf,df->gd/dot_general | solution.py:61
  148.0 0.0 all-reduce.2.cloned.1.call-update
  148.0 0.0 copy-start.8
  148.0 0.0 reduce-scatter.12.cloned.1.call-start
  148.1 196.8 %all-reduce.2.cloned.1.call-done = f32[256,3072]{1,0:T(8,128)} async-done(((f32[256,3072]{1,0:T(8,128)}), f32[256,3072]{1,0:T(8,128)}) %all-reduce.2.cloned.1.call-update) | async-done | bytes 3145744 | tf_op jit(solution)/shard_map/psum | solution.py:64
  344.8 4.6 multiply_convert_fusion
  349.4 6.6 %convolution_bitcast_fusion = f32[256,1024]{0,1:T(8,128)} fusion(bf16[256,256]{1,0:T(8,128)(2,1)S(1)} %copy-done.8, bf16[256,3072]{1,0:T(8,128)(2,1)} %multiply_convert_fusion, bf16[1024,3072]{1,0:T(8,128)(2,1)} %param.15, f32[256,1024]{1,0:T(8,128)S(1)} %copy-done.5), kind=kOutput, calls=%fused_computation.16 | convolution fusion | flops 1747189760 | bytes 10092544 | tf_op jit(solution)/shard_map/gz,gh->zh/dot_general | solution.py:21
  356.0 2.5 copy.22
  358.5 0.0 reduce-scatter.12.cloned.1.call-update
  358.6 0.0 reduce-scatter.8.cloned.1.call-start
  358.6 7.8 %fusion.28 = f32[1024,3072]{1,0:T(8,128)} fusion(bf16[256,3072]{1,0:T(8,128)(2,1)} %multiply_convert_fusion, f32[256,1024]{1,0:T(8,128)S(1)} %copy-done.5), kind=kOutput, calls=%fused_computation.39 | convolution fusion | flops 1611923456 | bytes 15204352 | tf_op jit(solution)/shard_map/gh,gd->hd/dot_general | solution.py:16
  366.4 0.0 reduce-scatter.8.cloned.1.call-update
  366.4 41.1 %psum.14 = f32[]{:T(128)} all-reduce(f32[]{:T(128)} %get-tuple-element.15), channel_id=1, replica_groups=mesh['dp'=16,'feat'=16] {'feat'}, use_global_device_ids=true, to_apply=%region_3.0 | all-reduce | flops 1 | bytes 8 | tf_op jit(solution)/shard_map/psum | solution.py:54
  408.2 14.2 %reduce-scatter.12.cloned.1.call-done = f32[16,1024]{1,0:T(8,128)} async-done(((f32[256,1024]{1,0:T(8,128)}), f32[16,1024]{1,0:T(8,128)}) %reduce-scatter.12.cloned.1.call-update) | async-done | bytes 65552
  422.4 86.0 %reduce-scatter.8.cloned.1.call-done = f32[64,3072]{1,0:T(8,128)} async-done(((f32[1024,3072]{1,0:T(8,128)}), f32[64,3072]{1,0:T(8,128)}) %reduce-scatter.8.cloned.1.call-update) | async-done | bytes 786448 | tf_op jit(solution)/shard_map/reduce_scatter | solution.py:70
  (21 shorter events, 0.1 us)
Async XLA Ops:
  7.2 1.7 copy-start
  7.2 13.8 %copy-start.10 = (s32[384]{0:T(512)S(1)}, s32[384]{0:T(512)}, u32[]{:S(2)}) copy-start(s32[384]{0:T(512)} %param.9) | copy-start | bytes 4612
  7.2 93.6 %reduce-scatter.10.cloned.1.call-start = ((), (), s32[]{:S(2)}) async-start(), calls=%async_computation.6 | async-start | bytes 557056
  28.1 6.4 %copy-start.6 = (bf16[256,1024]{1,0:T(8,128)(2,1)S(1)}, bf16[256,1024]{1,0:T(8,128)(2,1)}, u32[]{:S(2)}) copy-start(bf16[256,1024]{1,0:T(8,128)(2,1)} %param.14) | copy-start | bytes 1572868
  28.1 6.4 %copy-start.7 = (bf16[256,256]{1,0:T(8,128)(2,1)S(1)}, bf16[256,256]{1,0:T(8,128)(2,1)}, u32[]{:S(2)}) copy-start(bf16[256,256]{1,0:T(8,128)(2,1)} %param.12) | copy-start | bytes 393220
  34.4 101.9 %all-gather.2.cloned.1.call-start = ((), (), s32[]{:S(2)}) async-start(), calls=%async_computation.3 | async-start | bytes 1392640 | tf_op jit(solution)/shard_map/all_gather | solution.py:50
  34.5 6.3 %slice-start = ((s8[6291456]{0:T(1024)(128)(4,1)}), s8[4194304]{0:T(1024)(128)(4,1)S(1)}, s32[]{:S(2)}) async-start(s8[6291456]{0:T(1024)(128)(4,1)} %bitcast.21), calls=%async_computation.8 | async-start | bytes 8388608
  34.8 1.0 copy-start.4
  35.8 5.0 slice-start.1
  40.8 5.3 %copy-start.1 = (f32[256,3072]{1,0:T(8,128)}, f32[256,3072]{1,0:T(8,128)S(1)}, u32[]{:S(2)}) copy-start(f32[256,3072]{1,0:T(8,128)S(1)} %convolution_tanh_fusion) | copy-start | bytes 9437188
  40.8 6.3 %copy-start.9 = (s32[256]{0:T(256)S(1)}, s32[256]{0:T(256)}, u32[]{:S(2)}) copy-start(s32[256]{0:T(256)} %param.13) | copy-start | bytes 3076
  46.1 1.0 copy-start.2
  48.7 296.1 %all-reduce.2.cloned.1.call-start = ((), (), s32[]{:S(2)}) async-start(), calls=%async_computation.4 | async-start | bytes 6291456 | tf_op jit(solution)/shard_map/psum | solution.py:64
  138.7 2.8 copy-start.3
  148.0 201.5 %copy-start.5 = (f32[256,1024]{1,0:T(8,128)S(1)}, f32[256,1024]{1,0:T(8,128)}, u32[]{:S(2)}) copy-start(f32[256,1024]{1,0:T(8,128)} %copy-done.4) | copy-start | bytes 3145732
  148.0 201.4 %copy-start.8 = (bf16[256,256]{1,0:T(8,128)(2,1)S(1)}, bf16[256,256]{1,0:T(8,128)(2,1)}, u32[]{:S(2)}) copy-start(bf16[256,256]{1,0:T(8,128)(2,1)} %param.12) | copy-start | bytes 393220
  148.0 274.4 %reduce-scatter.12.cloned.1.call-start = ((), (), s32[]{:S(2)}) async-start(), calls=%async_computation.7 | async-start | bytes 1114112
  358.6 149.8 %reduce-scatter.8.cloned.1.call-start = ((), (), s32[]{:S(2)}) async-start(), calls=%async_computation.5 | async-start | bytes 13369344 | tf_op jit(solution)/shard_map/reduce_scatter | solution.py:70
Sparse Core Ops, SparseCore 0:
  34.5 66.1 reduce-scatter.9
  102.7 33.5 all-gather.1
  148.1 196.6 all-reduce.1
  358.7 63.6 reduce-scatter.11
  425.4 82.9 reduce-scatter.7
